TPU v7x, 128 devices: a whole 4x4x4 slice. The times are simulated.
128 devices in a mesh: row: 32 (over x, z, core), col: 4 (over y).
Axes of the slice: x: 4, y: 4, z: 4, core: 2. Of those that a mesh axis runs over, the one named last changes fastest.
Arguments:
- front: float32 [6, 32, 128, 16, 4, 128], P(None, 'row', None, None, 'col'), may hold values from -6 to 6
- mask: int32 [6, 32, 16, 4], P(None, 'row', None, 'col'), may hold values 0 or 1
- child_tiles: float32 [24576, 16384], P(('row', 'col')), may hold values from -6 to 6
- owner_map: int32 [24576, 1], P(('row', 'col')), may hold values from 0 to 127; in each aligned block of 192 rows (0 to 191, 192 to 383, ...) at most 2 rows name the same one
- parent_slot: int32 [24576], P(('row', 'col')), may hold values from 0 to 95
- pivot_order: int32 [512], replicated, may hold values from 0 to 511, each once
- inv_pivot: float32 [512, 512], replicated, as said below
Outputs:
- updated_front: float32 [6, 32, 128, 16, 4, 128], P(None, 'row', None, None, 'col')
Inputs may be any that keep to these rules, and one draw needn't show every extreme that they name: owner_map[t, 0] is the device r * 4 + c whose blocks receive tile t; among the 192 tiles of one device at most 2 name the same device, and exactly 2 do for some. parent_slot[t] is a 16 + b for the receiving device's local block (a, b). inv_pivot is symmetric.
All inputs are finite; a program needn't handle non-finite values. No bound on the sum of `mask` on one device may be relied on, other than what follows from the above.
Results may differ from a plain program's by a relative error of at most 0.00009.
Values sent between devices are 32-bit elements; how exact they have to be, the bound alone decides.
A program may use at most 192 MiB of HBM per device.

v0:
```python
import functools

import jax
import jax.numpy as jnp
from jax import lax
from jax.experimental import pallas as pl
from jax.experimental.pallas import tpu as pltpu
from jax.sharding import PartitionSpec as P

MOST = 2
CAP = 48
SLOTS = 4 * CAP
MESH = pl.DeviceIdType.MESH
F32 = jnp.float32
BF16 = jnp.bfloat16
GROUPS = ((8, 8, 8), (16, 12, 12), (12, 12, 16), (8, 8, 8))
N_GROUPS = len(GROUPS)
CHUNKS = []
SPANS = []
_row = 0
for _k, _sizes in enumerate(GROUPS):
    SPANS.append((_row, sum(_sizes)))
    for _p, _n in enumerate(_sizes):
        CHUNKS.append((_k, _p, _row, _n))
        _row += _n
N_CHUNKS = len(CHUNKS)
AXES = ((0, 1, 2), (1, 2, 0), (2, 0, 1))


def exchange_kernel(
    child, front, owner, slot, mask_row, out, panel, trail, flag,
    buf, recv1, recv2, recv3, sib, fbuf, pan, tabs, mown, mcore, mtwo, mx, mfour, mz, my,
    hsend, hrecv, fsend, frecv,
    child_sem, front_sem, out_sem, send_sem, recv_sem, sib_ssem, sib_rsem,
    m_ssem, m_rsem, h_ssem, h_rsem, f_ssem, f_rsem,
    pan_sem, y_ssem, y_rsem, a_ssem, a_rsem, b_ssem, b_rsem, c_ssem, c_rsem,
):
    row_at, y = lax.axis_index("row"), lax.axis_index("col")
    x, z, core = row_at // 8, (row_at // 2) % 4, row_at % 2

    def peer(axis, shift):
        if axis == 0:
            return (((x + shift) % 4) * 8 + z * 2 + core, y)
        if axis == 1:
            return (x * 8 + ((z + shift) % 4) * 2 + core, y)
        return (row_at, (y + shift) % 4)

    sibling = (row_at + 1 - 2 * core, y)
    here = (x, z, y)

    def remote(src, dst, ssem, rsem, to):
        return pltpu.make_async_remote_copy(
            src_ref=src, dst_ref=dst, send_sem=ssem, recv_sem=rsem, device_id=to, device_id_type=MESH
        )

    front_in = pltpu.make_async_copy(front, fbuf, front_sem)
    for n, (_, _, r0, rows) in enumerate(CHUNKS):

        def load(g, carry, n=n, r0=r0, rows=rows):
            pltpu.make_async_copy(
                child.at[g, pl.ds(r0, rows)],
                buf.at[pl.ds(r0, rows), pl.ds(pl.multiple_of(g * 8, 8), 8), :],
                child_sem.at[n],
            ).start()
            return carry

        lax.fori_loop(0, SLOTS // 8, load, 0)
    front_in.start()

    barrier = pltpu.get_barrier_semaphore()
    for axis in range(3):
        for shift in (1, 2, 3):
            pl.semaphore_signal(barrier, inc=1, device_id=peer(axis, shift), device_id_type=MESH)
    pl.semaphore_signal(barrier, inc=1, device_id=sibling, device_id_type=MESH)
    pl.semaphore_wait(barrier, 10)

    sub8 = lax.broadcasted_iota(jnp.int32, (8, 128), 0)
    mown[...] = jnp.where(sub8 == x * 2 + core, jnp.broadcast_to(mask_row[0:1, :], (8, 128)), 0.0)
    copy = remote(mown, mcore, m_ssem.at[0], m_rsem.at[0], sibling)
    copy.start()
    copy.wait()
    mtwo[...] = mown[...] + mcore[...]
    copies = [
        remote(mtwo, mx.at[s - 1], m_ssem.at[s], m_rsem.at[s], peer(0, s)) for s in (1, 2, 3)
    ]
    for c in copies:
        c.start()
    for c in copies:
        c.wait()
    mfour[...] = mtwo[...] + mx[0] + mx[1] + mx[2]
    mz[pl.ds(z, 1)] = mfour[...].reshape(1, 8, 128)
    for s in (1, 2, 3):
        remote(mfour, mz.at[z], m_ssem.at[3 + s], m_rsem.at[3 + s], peer(1, s)).start()
    for s in (1, 2, 3):
        remote(mfour, mz.at[(z + 4 - s) % 4], m_ssem.at[3 + s], m_rsem.at[3 + s], peer(1, s)).wait()
    my[pl.ds(y, 1)] = mz[...].reshape(1, 4, 8, 128)
    for s in (1, 2, 3):
        remote(mz, my.at[y], m_ssem.at[6 + s], m_rsem.at[6 + s], peer(2, s)).start()
    for s in (1, 2, 3):
        remote(mz, my.at[(y + 4 - s) % 4], m_ssem.at[6 + s], m_rsem.at[6 + s], peer(2, s)).wait()
    masks = my[...].reshape(128, 128).astype(BF16)

    own = owner[...]
    at = slot[...]
    e = (own & 3) * 32 + ((own >> 3) & 3) * 8 + ((own >> 5) & 3) * 2 + ((own >> 2) & 1)
    lanes = lax.broadcasted_iota(jnp.int32, (SLOTS, 128), 1)
    by_owner = jnp.where(e == lanes, 1.0, 0.0).astype(BF16)
    keeps = jnp.dot(by_owner, masks, preferred_element_type=F32)
    keep = jnp.sum(jnp.where(at == lanes, keeps, 0.0), axis=1, keepdims=True)
    keep = jnp.where((at & 15) == 0, 1.0, keep)
    code = jnp.where(keep > 0.5, (e * 128 + at).astype(F32), -1.0)

    sub = lax.broadcasted_iota(jnp.int32, (SLOTS, SLOTS), 0)
    lan = lax.broadcasted_iota(jnp.int32, (SLOTS, SLOTS), 1)
    eye = sub == lan
    sub_f = sub.astype(F32)

    def to_row(col):
        return jnp.sum(jnp.where(eye, col, 0.0), axis=0, keepdims=True)

    def axis_shift(m, axis):
        digit = (m.astype(jnp.int32) >> (8, 10, 12)[axis]) & 3
        return ((digit + 4 - here[axis]) & 3).astype(F32)

    def route(col, axis):
        line = to_row(col)
        twin = jnp.max(jnp.where((col == line) & (sub < lan), 1.0, 0.0), axis=0, keepdims=True)
        first = (line >= 0.0) & (twin < 0.5)
        shift_col, shift_line = axis_shift(col, axis), axis_shift(line, axis)
        ahead = first & (shift_line == shift_col) & (line < col)
        rank = jnp.sum(jnp.where(ahead, 1.0, 0.0), axis=1, keepdims=True)
        place = jnp.where((col >= 0.0) & (rank < CAP), shift_col * CAP + rank, -1.0)
        over = jnp.max(jnp.where((col >= 0.0) & (rank >= CAP), 1.0, 0.0), axis=0, keepdims=True)
        goes = sub_f == to_row(place)
        passed = jnp.max(jnp.where(goes, line, -1.0), axis=1, keepdims=True)
        return jnp.where(goes, 1.0, 0.0).astype(BF16), passed, over

    def send_header(phase, p, passed):
        hsend[phase, p] = jnp.broadcast_to(passed, (SLOTS, 128))
        for s in (1, 2, 3):
            remote(
                hsend.at[phase, p, pl.ds(s * CAP, CAP)],
                hrecv.at[phase, p, pl.ds((s - 1) * CAP, CAP)],
                h_ssem.at[phase, p],
                h_rsem.at[phase, p],
                peer(AXES[p][phase], s),
            ).start()

    def take_header(phase, p):
        remote(
            hsend.at[phase, p, pl.ds(CAP, 3 * CAP)],
            hrecv.at[phase, p],
            h_ssem.at[phase, p],
            h_rsem.at[phase, p],
            peer(AXES[p][phase], 1),
        ).wait()
        return jnp.concatenate([hsend[phase, p, 0:CAP, 0:1], hrecv[phase, p, :, 0:1]], axis=0)

    overs = []
    for p in range(3):
        table, passed, over = route(code, AXES[p][0])
        tabs[0, p] = table
        overs.append(over)
        send_header(0, p, passed)

    def later_tables(phase):
        for p in range(3):
            table, passed, over = route(take_header(phase - 1, p), AXES[p][phase])
            tabs[phase, p] = table
            overs.append(over)
            send_header(phase, p, passed)

    def last_tables():
        for p in range(3):
            col = take_header(2, p)
            whole = col.astype(jnp.int32)
            block = (whole & 127) + jnp.where(((whole >> 7) & 1) == core, 96, 0)
            block = jnp.where(col >= 0.0, block.astype(F32), -1.0)
            tabs[3, p] = jnp.where(sub_f == to_row(block), 1.0, 0.0).astype(BF16)

    def split_dot(table, values):
        high = values.astype(BF16)
        low = (values - high.astype(F32)).astype(BF16)
        return jnp.dot(table, high, preferred_element_type=F32) + jnp.dot(
            table, low, preferred_element_type=F32
        )

    recvs = (None, recv1, recv2, recv3)

    def rows_of(phase, i):
        if phase == 0:
            return buf[i]
        return jnp.concatenate([buf[i, 0:CAP, :], recvs[phase][i]], axis=0)

    def chunk_wait(phase, n, r0, rows):
        if phase == 0:
            pltpu.make_async_copy(
                buf.at[pl.ds(r0, rows)], buf.at[pl.ds(r0, rows)], child_sem.at[n]
            ).wait()
        else:
            ref = recvs[phase].at[pl.ds(r0, rows)]
            remote(ref, ref, send_sem.at[phase - 1, n], recv_sem.at[phase - 1, n], sibling).wait_recv()

    def forward(phase, n):
        _, p, r0, rows = CHUNKS[n]
        chunk_wait(phase, n, r0, rows)
        table = tabs[phase, p]

        def body(it, carry):
            for h in range(2):
                i = r0 + it * 4 + h * 2
                both = jnp.concatenate([rows_of(phase, i), rows_of(phase, i + 1)], axis=1)
                got = split_dot(table, both)
                for k in range(2):
                    part = got[:, k * 128:(k + 1) * 128]
                    if phase == 0:
                        buf[i + k] = part
                    else:
                        buf[i + k, 0:CAP, :] = part[0:CAP]
                        recvs[phase][i + k] = part[CAP:]
            return carry

        lax.fori_loop(0, rows // 4, body, 0)
        for s in (1, 2, 3):
            if phase == 0:
                src = buf.at[pl.ds(r0, rows), pl.ds(s * CAP, CAP), :]
            else:
                src = recvs[phase].at[pl.ds(r0, rows), pl.ds((s - 1) * CAP, CAP), :]
            remote(
                src,
                recvs[phase + 1].at[pl.ds(r0, rows), pl.ds((s - 1) * CAP, CAP), :],
                send_sem.at[phase, n],
                recv_sem.at[phase, n],
                peer(AXES[p][phase], s),
            ).start()

    def finish(n):
        _, p, r0, rows = CHUNKS[n]
        chunk_wait(3, n, r0, rows)
        table = tabs[3, p]

        def body(it, carry):
            for h in range(2):
                i = r0 + it * 4 + h * 2
                both = jnp.concatenate([rows_of(3, i), rows_of(3, i + 1)], axis=1)
                got = split_dot(table, both)
                for k in range(2):
                    part = got[:, k * 128:(k + 1) * 128]
                    recv3[i + k, 0:96, :] = part[0:96]
                    for a in range(6):
                        fbuf[a, i + k] = fbuf[a, i + k] + part[96 + a * 16:112 + a * 16]
            return carry

        lax.fori_loop(0, rows // 4, body, 0)
        remote(
            recv3.at[pl.ds(r0, rows), pl.ds(0, 96), :],
            sib.at[pl.ds(r0, rows)],
            sib_ssem.at[n],
            sib_rsem.at[n],
            sibling,
        ).start()

    def from_sibling(n):
        _, p, r0, rows = CHUNKS[n]
        ref = sib.at[pl.ds(r0, rows)]
        remote(ref, ref, sib_ssem.at[n], sib_rsem.at[n], sibling).wait_recv()

        def body(it, carry):
            i = r0 + it
            got = sib[i]
            for a in range(6):
                fbuf[a, i] = fbuf[a, i] + got[a * 16:a * 16 + 16]
            return carry

        lax.fori_loop(0, rows, body, 0)
        pltpu.make_async_copy(
            fbuf.at[:, pl.ds(r0, rows)], out.at[:, pl.ds(r0, rows)], out_sem.at[n]
        ).start()

    holds = core == y % 2
    on_line = z % 2 == y // 2
    mine = 2 * x + z // 2
    other = 2 * x + ((z + 2) % 4) // 2
    lower = 2 * x
    source = jnp.logical_and(holds, on_line)
    off_line = jnp.logical_and(holds, jnp.logical_not(on_line))

    def pan_copy(g):
        r0, rows = SPANS[g]
        return pltpu.make_async_copy(
            pan.at[:, pl.ds(r0, rows)], panel.at[y, :, pl.ds(r0, rows)], pan_sem.at[g]
        )

    def y_copy(g, s, at):
        r0, rows = SPANS[g]
        return remote(
            pan.at[:, pl.ds(r0, rows)], panel.at[at, :, pl.ds(r0, rows)],
            y_ssem.at[g, s - 1], y_rsem.at[g, s - 1], peer(2, s),
        )

    def panel_out(g):
        r0, rows = SPANS[g]

        def body(it, carry):
            i = pl.multiple_of(r0 + it * 4, 4)
            for a in range(6):
                for k in range(4):
                    pan[a, pl.ds(i + k, 1), :] = fbuf[a, i + k, 0:1, :]
            return carry

        lax.fori_loop(0, rows // 4, body, 0)
        pan_copy(g).start()
        for s in (1, 2, 3):
            y_copy(g, s, y).start()

    def trail_at(g, place, half):
        r0, rows = SPANS[g]
        return trail.at[place, :, half, pl.ds(r0, rows)]

    def source_copy(g, half, sems, s, place):
        r0, rows = SPANS[g]
        return remote(
            panel.at[:, half, pl.ds(r0, rows)], trail_at(g, place, half),
            sems[0].at[g, 0, s - 1], sems[1].at[g, 0, s - 1], peer(half, s),
        )

    def own_copy(g, half):
        r0, rows = SPANS[g]
        return pltpu.make_async_copy(
            panel.at[:, half, pl.ds(r0, rows)], trail_at(g, mine, half), pan_sem.at[N_GROUPS + half * N_GROUPS + g]
        )

    a_sems, b_sems = (a_ssem, a_rsem), (b_ssem, b_rsem)

    def from_x(s):
        return 2 * ((x + 4 - s) % 4)

    def panel_rows(g):
        pan_copy(g).wait()
        for s in (1, 2, 3):
            y_copy(g, s, (y + 4 - s) % 4).wait_recv()

        @pl.when(source)
        def _():
            for half in (0, 1):
                own_copy(g, half).start()
                for s in (1, 2, 3):
                    source_copy(g, half, (a_sems, b_sems)[half], s, mine).start()

    def a_line(g, s, i, base):
        place = 2 * i + base // 2
        ref = trail_at(g, place, 0)
        return remote(ref, ref, a_ssem.at[g, 1 + i, s - 1], a_rsem.at[g, 1 + i, s - 1], peer(1, s))

    def b_line(g, s, zz, at):
        ref = trail_at(g, 2 * at + zz, 1)
        return remote(ref, ref, b_ssem.at[g, 1 + zz, s - 1], b_rsem.at[g, 1 + zz, s - 1], peer(0, s))

    def panel_lines(g):
        @pl.when(source)
        def _():
            for half in (0, 1):
                own_copy(g, half).wait()
            for s in (1, 2, 3):
                source_copy(g, 0, a_sems, s, from_x(s) + z // 2).wait_recv()
            for i in range(4):
                for s in (1, 3, 2):
                    a_line(g, s, i, z).start()
            source_copy(g, 1, b_sems, 2, other).wait_recv()

        @pl.when(off_line)
        def _():
            for s in (1, 3):
                source_copy(g, 1, b_sems, s, lower + ((z + 4 - s) % 4) // 2).wait_recv()

        @pl.when(holds)
        def _():
            for zz in (0, 1):
                for s in (1, 2, 3):
                    b_line(g, s, zz, x).start()

    def to_sibling(g):
        r0, rows = SPANS[g]
        ref = trail.at[:, :, :, pl.ds(r0, rows)]
        return remote(ref, ref, c_ssem.at[g], c_rsem.at[g], sibling)

    def panel_cores(g):
        @pl.when(source)
        def _():
            for i in range(4):
                a_line(g, 2, i, (z + 2) % 4).wait_recv()

        @pl.when(off_line)
        def _():
            for i in range(4):
                for s in (1, 3):
                    a_line(g, s, i, (z + 4 - s) % 4).wait_recv()

        @pl.when(holds)
        def _():
            for zz in (0, 1):
                for s in (1, 2, 3):
                    b_line(g, s, zz, (x + 4 - s) % 4).wait_recv()
            to_sibling(g).start()

    def panel_end(g):
        for s in (1, 2, 3):
            y_copy(g, s, y).wait_send()

        @pl.when(source)
        def _():
            for half in (0, 1):
                for s in (1, 2, 3):
                    source_copy(g, half, (a_sems, b_sems)[half], s, mine).wait_send()
            for i in range(4):
                for s in (1, 2, 3):
                    a_line(g, s, i, z).wait_send()

        @pl.when(holds)
        def _():
            for zz in (0, 1):
                for s in (1, 2, 3):
                    b_line(g, s, zz, x).wait_send()
            to_sibling(g).wait_send()

        @pl.when(jnp.logical_not(holds))
        def _():
            to_sibling(g).wait_recv()

    def flag_copies(step):
        return [
            remote(fsend.at[step], frecv.at[step, s - 1], f_ssem.at[step, s - 1],
                   f_rsem.at[step, s - 1], peer(step, s))
            for s in (1, 2, 3)
        ]

    flag_last = remote(fsend.at[3], frecv.at[3, 0], f_ssem.at[3, 0], f_rsem.at[3, 0], sibling)

    def flag_step(step):
        if step > 0:
            for c in flag_copies(step - 1):
                c.wait()
            fsend[step] = (
                fsend[step - 1] + frecv[step - 1, 0] + frecv[step - 1, 1] + frecv[step - 1, 2]
            )
        for c in flag_copies(step) if step < 3 else [flag_last]:
            c.start()

    flags_done = 0
    steps = sorted((stage + g, stage, g) for stage in range(8) for g in range(N_GROUPS))
    for _, stage, g in steps:
        chunks = [n for n in range(N_CHUNKS) if CHUNKS[n][0] == g]
        if stage < 3:
            if g == 0 and stage > 0:
                later_tables(stage)
            for n in chunks:
                forward(stage, n)
        elif stage == 3:
            if g == 0:
                last_tables()
                total = overs[0]
                for o in overs[1:]:
                    total = jnp.maximum(total, o)
                fsend[0] = jnp.broadcast_to(total, (8, 128))
                front_in.wait()
            for n in chunks:
                finish(n)
        elif stage == 4:
            for n in chunks:
                from_sibling(n)
            panel_out(g)
        elif stage == 5:
            panel_rows(g)
        elif stage == 6:
            panel_lines(g)
        else:
            panel_cores(g)
        if stage >= 3 and flags_done < 4:
            flag_step(flags_done)
            flags_done += 1
    flag_last.wait()
    flag[...] = fsend[3] + frecv[3, 0]
    for n, (_, _, r0, rows) in enumerate(CHUNKS):
        for phase in range(3):
            ref = recvs[phase + 1].at[pl.ds(r0, rows)]
            remote(ref, ref, send_sem.at[phase, n], recv_sem.at[phase, n], sibling).wait_send()
        ref = sib.at[pl.ds(r0, rows)]
        remote(ref, ref, sib_ssem.at[n], sib_rsem.at[n], sibling).wait_send()
        pltpu.make_async_copy(
            fbuf.at[:, pl.ds(r0, rows)], out.at[:, pl.ds(r0, rows)], out_sem.at[n]
        ).wait()
    for g in range(N_GROUPS):
        panel_end(g)


def exchange(child, front, owner, slot, mask_row):
    dma = pltpu.SemaphoreType.DMA
    vmem = pl.BlockSpec(memory_space=pltpu.VMEM)
    hbm = pl.BlockSpec(memory_space=pl.ANY)
    return pl.pallas_call(
        exchange_kernel,
        out_shape=(
            jax.ShapeDtypeStruct((6, 128, 16, 128), F32),
            jax.ShapeDtypeStruct((4, 6, 128, 128), F32),
            jax.ShapeDtypeStruct((8, 4, 2, 128, 128), F32),
            jax.ShapeDtypeStruct((8, 128), F32),
        ),
        in_specs=[hbm, hbm, vmem, vmem, vmem],
        out_specs=(hbm, hbm, hbm, vmem),
        scratch_shapes=[
            pltpu.VMEM((128, SLOTS, 128), F32),
            pltpu.VMEM((128, 3 * CAP, 128), F32),
            pltpu.VMEM((128, 3 * CAP, 128), F32),
            pltpu.VMEM((128, 3 * CAP, 128), F32),
            pltpu.VMEM((128, 96, 128), F32),
            pltpu.VMEM((6, 128, 16, 128), F32),
            pltpu.VMEM((6, 128, 128), F32),
            pltpu.VMEM((4, 3, SLOTS, SLOTS), BF16),
            pltpu.VMEM((8, 128), F32),
            pltpu.VMEM((8, 128), F32),
            pltpu.VMEM((8, 128), F32),
            pltpu.VMEM((3, 8, 128), F32),
            pltpu.VMEM((8, 128), F32),
            pltpu.VMEM((4, 8, 128), F32),
            pltpu.VMEM((4, 4, 8, 128), F32),
            pltpu.VMEM((3, 3, SLOTS, 128), F32),
            pltpu.VMEM((3, 3, 3 * CAP, 128), F32),
            pltpu.VMEM((4, 8, 128), F32),
            pltpu.VMEM((4, 3, 8, 128), F32),
            dma((N_CHUNKS,)),
            dma,
            dma((N_CHUNKS,)),
            dma((3, N_CHUNKS)),
            dma((3, N_CHUNKS)),
            dma((N_CHUNKS,)),
            dma((N_CHUNKS,)),
            dma((10,)),
            dma((10,)),
            dma((3, 3)),
            dma((3, 3)),
            dma((4, 3)),
            dma((4, 3)),
            dma((3 * N_GROUPS,)),
            dma((N_GROUPS, 3)),
            dma((N_GROUPS, 3)),
            dma((N_GROUPS, 5, 3)),
            dma((N_GROUPS, 5, 3)),
            dma((N_GROUPS, 3, 3)),
            dma((N_GROUPS, 3, 3)),
            dma((N_GROUPS,)),
            dma((N_GROUPS,)),
        ],
        compiler_params=pltpu.CompilerParams(
            collective_id=0, has_side_effects=True, vmem_limit_bytes=62 * 2**20
        ),
        name="tile_exchange",
    )(child, front, owner, slot, mask_row)


def schur_kernel(
    col_at, mask, order, inverse, panel, trail, front, out,
    n_high, n_low, m_high, m_low, t_high, t_low,
):
    def split(values):
        high = values.astype(BF16)
        return high, (values - high.astype(F32)).astype(BF16)

    def dot(a, b):
        return jnp.dot(a, b, preferred_element_type=F32)

    def dot_t(a, b):
        return lax.dot_general(a, b, (((1,), (1,)), ((), ())), preferred_element_type=F32)

    def three(left, right, how):
        return how(left[0], right[0]) + how(left[0], right[1]) + how(left[1], right[0])

    @pl.when(pl.program_id(0) == 0)
    def _():
        sub = lax.broadcasted_iota(jnp.int32, (512, 512), 0)
        place = jnp.where(sub == order[...], 1.0, 0.0).astype(BF16)
        for part, n_ref, m_ref in zip(split(inverse[...]), (n_high, n_low), (m_high, m_low)):
            rows = dot(place, part).astype(BF16)
            n_ref[...] = rows
            m_ref[...] = dot_t(rows, place).astype(BF16)
        for half in range(2):
            for m in range(8):
                for k in range(4):
                    high, low = split(trail[m, k, half])
                    t_high[half * 8 + m, :, k * 128:(k + 1) * 128] = high
                    t_low[half * 8 + m, :, k * 128:(k + 1) * 128] = low

    pair = pl.program_id(0)
    rows = jnp.concatenate(
        [jnp.concatenate([panel[k, a] for k in range(4)], axis=1) for a in range(2)], axis=0
    )
    rows = split(rows)
    mine = pl.ds(pl.multiple_of(col_at[0] * 128, 128), 128)
    factor = three(rows, (n_high[:, mine], n_low[:, mine]), dot)
    turned = split(three(rows, (m_high[...], m_low[...]), dot))
    for a in range(2):
        out[pl.ds(a * 2048, 128, stride=16), :] = factor[a * 128:(a + 1) * 128]
    for first in range(0, 16, 2):
        cols = (
            t_high[first:first + 2].reshape(256, 512),
            t_low[first:first + 2].reshape(256, 512),
        )
        update = three(turned, cols, dot_t)
        for b in (first, first + 1):
            if b == 0:
                continue
            for a in range(2):
                at = pl.ds(a * 2048 + b, 128, stride=16)
                part = update[a * 128:(a + 1) * 128, (b - first) * 128:(b - first + 1) * 128]
                keep = mask[pair * 2 + a, b] > 0
                out[at, :] = jnp.where(keep, front[at, :] - part, 0.0)


def finish_front(col_at, mask, order, inverse, panel, trail, assembled):
    smem = pl.BlockSpec(memory_space=pltpu.SMEM)
    return pl.pallas_call(
        schur_kernel,
        grid=(3,),
        out_shape=jax.ShapeDtypeStruct((12288, 128), F32),
        in_specs=[
            smem,
            smem,
            pl.BlockSpec((1, 512), lambda i: (0, 0)),
            pl.BlockSpec((512, 512), lambda i: (0, 0)),
            pl.BlockSpec((4, 2, 128, 128), lambda i: (0, i, 0, 0)),
            pl.BlockSpec((8, 4, 2, 128, 128), lambda i: (0, 0, 0, 0, 0)),
            pl.BlockSpec((4096, 128), lambda i: (i, 0)),
        ],
        out_specs=pl.BlockSpec((4096, 128), lambda i: (i, 0)),
        scratch_shapes=[
            pltpu.VMEM((512, 512), BF16),
            pltpu.VMEM((512, 512), BF16),
            pltpu.VMEM((512, 512), BF16),
            pltpu.VMEM((512, 512), BF16),
            pltpu.VMEM((16, 128, 512), BF16),
            pltpu.VMEM((16, 128, 512), BF16),
        ],
        compiler_params=pltpu.CompilerParams(vmem_limit_bytes=40 * 2**20),
        name="schur",
    )(col_at, mask, order, inverse, panel, trail, assembled)


def any_front(front, mask, child_tiles, owner_map, parent_slot, pivot_order, inv_pivot):
    n_row = lax.axis_size("row")
    n_col = lax.axis_size("col")
    devices = n_row * n_col
    blk_rows = front.shape[0]
    block_size = front.shape[2]
    blk_cols = front.shape[3]
    rows_here = blk_rows * block_size
    local_width = blk_cols * block_size
    panel_size = inv_pivot.shape[0]
    panel_local = panel_size // (block_size * n_col)
    slots_total = blk_rows * blk_cols
    tile_area = child_tiles.shape[1]
    owner_dev = owner_map[:, 0]
    owner_hits = (owner_dev[:, None] == jnp.arange(devices, dtype=jnp.int32)[None, :]).astype(
        jnp.int32
    )
    earlier = jnp.cumsum(owner_hits, axis=0) - owner_hits
    tile_rank = jnp.sum(earlier * owner_hits, axis=1)
    send_slot = owner_dev * MOST + tile_rank
    outgoing = jnp.zeros((devices * MOST, tile_area), jnp.float32).at[send_slot].set(child_tiles)
    targets = jnp.full((devices * MOST,), slots_total, jnp.int32).at[send_slot].set(parent_slot)
    arrived, places = (
        lax.all_to_all(
            outgoing.reshape(devices, MOST, tile_area),
            ("row", "col"),
            split_axis=0,
            concat_axis=0,
            tiled=True,
        ),
        lax.all_to_all(
            targets.reshape(devices, MOST), ("row", "col"), split_axis=0, concat_axis=0, tiled=True
        ),
    )
    arrived = arrived.reshape(devices * MOST, tile_area)
    places = places.reshape(devices * MOST)
    blocks = jnp.zeros((slots_total, tile_area), jnp.float32).at[places].add(arrived, mode="drop")
    contrib = (
        blocks.reshape(blk_rows, blk_cols, block_size, block_size)
        .transpose(0, 2, 1, 3)
        .reshape(rows_here, local_width)
    )
    assembled = front.reshape(rows_here, local_width) + contrib
    own_panel = assembled[:, : panel_local * block_size]
    gathered = lax.all_gather(own_panel, "col", axis=1, tiled=True)
    panel_cols = (
        gathered.reshape(rows_here, n_col, panel_local, block_size)
        .transpose(0, 2, 1, 3)
        .reshape(rows_here, panel_size)
    )
    permuted = jnp.take(panel_cols, pivot_order, axis=1)
    factor = jnp.dot(permuted, inv_pivot, precision=lax.Precision.HIGHEST)
    col_here = lax.axis_index("col")
    window_local = blk_cols * n_col // n_row
    window_mine = permuted[: window_local * block_size]
    everything = lax.all_gather(window_mine, "row", axis=0, tiled=True).reshape(
        n_row, window_local, block_size, panel_size
    )
    block_index = jnp.arange(blk_cols, dtype=jnp.int32) * n_col + col_here
    needed = everything[block_index % n_row, block_index // n_row]
    needed = needed.reshape(blk_cols * block_size, panel_size)
    trailing = needed[panel_local * block_size :]
    update = jnp.einsum("rp,cp->rc", factor, trailing, precision=lax.Precision.HIGHEST)
    keep_block = mask.reshape(blk_rows, blk_cols)[:, panel_local:] > 0
    schur_part = (assembled[:, panel_local * block_size :] - update).reshape(
        blk_rows, block_size, blk_cols - panel_local, block_size
    )
    schur_part = jnp.where(keep_block[:, None, :, None], schur_part, 0.0)
    factor_mine = lax.dynamic_slice_in_dim(
        factor.reshape(rows_here, panel_local, n_col, block_size), col_here, 1, 2
    ).reshape(rows_here, panel_local * block_size)
    result = jnp.concatenate(
        [factor_mine, schur_part.reshape(rows_here, (blk_cols - panel_local) * block_size)], 1
    )
    return result.reshape(front.shape)


def per_device(front, mask, child_tiles, owner_map, parent_slot, pivot_order, inv_pivot):
    child4 = child_tiles.reshape(24, 8, 128, 128).transpose(0, 2, 1, 3)
    mask_here = mask.reshape(6, 16)
    mask_row = jnp.pad(mask.reshape(1, 96).astype(F32), ((0, 7), (0, 32)))
    assembled, panel, trail, flag = exchange(
        child4,
        front.reshape(6, 128, 16, 128),
        owner_map.reshape(192, 1),
        parent_slot.reshape(192, 1),
        mask_row,
    )
    col_at = lax.axis_index("col").astype(jnp.int32).reshape(1)
    return lax.cond(
        flag[0, 0] > 0.5,
        lambda: any_front(
            front, mask, child_tiles, owner_map, parent_slot, pivot_order, inv_pivot
        ),
        lambda: finish_front(
            col_at,
            mask_here,
            pivot_order.reshape(1, 512),
            inv_pivot,
            panel,
            trail,
            assembled.reshape(12288, 128),
        ).reshape(front.shape),
    )


def solution(mesh):
    placed = (
        P(None, "row", None, None, "col", None),
        P(None, "row", None, "col"),
        P(("row", "col"), None),
        P(("row", "col"), None),
        P(("row", "col")),
        P(),
        P(),
    )
    return jax.shard_map(
        per_device,
        mesh=mesh,
        in_specs=placed,
        out_specs=P(None, "row", None, None, "col", None),
        check_vma=False,
    )
```

profile of v0, /device:TPU:1, one launch (start us, length us, event | category | flops | bytes accessed | tf_op | source)
XLA Modules:
  0.0 247.9 jit_solution(3462241380404595441)
XLA Ops:
  6.5 1.4 copy.48.owner
  8.0 1.4 copy.49.slot
  9.4 0.7 convert_reduce_fusion
  10.1 0.1 convert_element_type.27
  10.2 0.6 pad.8.mask_row
  10.8 0.0 copy-start.2
  10.8 0.0 copy-start.4
  10.8 0.0 copy-start.5
  10.8 0.0 copy-start.6
  10.8 211.9 %tile_exchange.1 = (f32[6,128,16,128]{3,2,1,0:T(8,128)}, f32[4,6,128,128]{3,2,1,0:T(8,128)}, f32[8,4,2,128,128]{4,3,2,1,0:T(8,128)}, f32[8,128]{1,0:T(8,128)}) custom-call(f32[24,128,8,128]{3,2,1,0:T(8,128)} %bitcast.80, f32[6,128,16,128]{3,2,1,0:T(8,128)} %bitcast.73, s32[192,1]{1,0:T(8,128)} %copy.48.owner, s32[192,1]{1,0:T(8,128)} %copy.49.slot, ...), custom_call_target="tpu_custom_call" | custom-call | tf_op jit(solution)/shard_map/tile_exchange/pallas_call | solution.py:500
  222.7 1.2 slice.30
  224.5 0.0 copy-done.2
  224.5 0.0 copy-done.4
  224.6 0.0 copy-done.5
  224.6 0.0 copy-done.6
  224.6 16.5 %conditional.1 = (f32[6,1,128,16,1,128]{5,3,2,0,4,1:T(8,128)}) conditional(s32[]{:T(128)} %bitcast.27, (s32[512]{0:T(512)S(1)}, f32[6,128,16,128]{3,2,1,0:T(8,128)}, s32[]{:T(128)}, s32[6,1,16,1]{2,3,1,0:T(1,128)S(1)}, f32[512,512]{1,0:T(8,128)S(1)}, /*index=5*/f32[4,6,128,128]{3,2,1,0:T(8,128)}, f32[8,4,2,128,128]{4,3,2,1,0:T(8,128)}) %tuple.33, ...), branch_computations={%region_0.1_spmd, %region_1.8_spmd} | conditional | flops 11491074048 | bytes 445776736 | solution.py:736
  224.6 16.3 %schur.1 = f32[12288,128]{1,0:T(8,128)} custom-call(s32[1]{0:T(128)} %bitcast.col_at, s32[6,16]{1,0:T(8,128)S(1)} %bitcast.68, s32[1,512]{1,0:T(1,128)S(1)} %bitcast.89, f32[512,512]{1,0:T(8,128)S(1)} %get-tuple-element.39.inverse, f32[4,6,128,128]{3,2,1,0:T(8,128)} %get-tuple-element.40.panel, f32[8,4,2,128,128]{4,3,2,1,0:T(8,128)} %get-tuple-element.41.trail, ...), custom_call_target="tpu_custom_call" | custom-call | tf_op jit(solution)/shard_map/cond/branch_0_fun/schur/pallas_call | solution.py:620
  (1 shorter events, 0.0 us)
Async XLA Ops:
  10.8 213.7 %copy-start.2 = (f32[512,512]{1,0:T(8,128)S(1)}, f32[512,512]{1,0:T(8,128)}, u32[]{:S(2)}) copy-start(f32[512,512]{1,0:T(8,128)} %param.15) | copy-start | bytes 3145732
  10.8 213.7 %copy-start.4 = (s32[6,1,16,1]{2,3,1,0:T(1,128)S(1)}, s32[6,1,16,1]{2,3,1,0:T(1,128)}, u32[]{:S(2)}) copy-start(s32[6,1,16,1]{2,3,1,0:T(1,128)} %param.10) | copy-start | bytes 1156
  10.8 213.8 %copy-start.5 = (s32[512]{0:T(512)S(1)}, s32[512]{0:T(512)}, u32[]{:S(2)}) copy-start(s32[512]{0:T(512)} %param.14) | copy-start | bytes 6148
  10.8 213.8 %copy-start.6 = (s32[192,1]{0,1:T(1,128)S(1)}, s32[192,1]{0,1:T(1,128)}, u32[]{:S(2)}) copy-start(s32[192,1]{0,1:T(1,128)} %param.12) | copy-start | bytes 2308
where the time goes:
time: 248 us
  Pallas kernels  228 us (92%)
  between operations  14.1 us (6%)
  local copies, waits for them, and re-layouts  4.76 us (2%)
    pallas_call x1, Pallas kernels, exchange(): pl.pallas_call(exchange_kernel, out_shape=(jax.ShapeDtypeStruct((6, 128,...  212 us
    pallas_call x1, Pallas kernels, finish_front(): pl.pallas_call(schur_kernel, grid=(3,), out_shape=jax.ShapeDtypeStruct((1...  16.3 us

commit v1 on v0

--- a/solution.py
+++ b/solution.py
@@ -13,7 +13,7 @@
 MESH = pl.DeviceIdType.MESH
 F32 = jnp.float32
 BF16 = jnp.bfloat16
-GROUPS = ((8, 8, 8), (16, 12, 12), (12, 12, 16), (8, 8, 8))
+GROUPS = ((6, 4, 6), (4, 6, 6), (8, 8, 8), (8, 8, 8), (6, 4, 6), (4, 6, 6), (6, 6, 4))
 N_GROUPS = len(GROUPS)
 CHUNKS = []
 SPANS = []
@@ -28,8 +28,8 @@
 
 
 def exchange_kernel(
-    child, front, owner, slot, mask_row, out, panel, trail, flag,
-    buf, recv1, recv2, recv3, sib, fbuf, pan, tabs, mown, mcore, mtwo, mx, mfour, mz, my,
+    child, front, owner, slot, mask, out, panel, trail, flag,
+    buf, recv1, recv2, recv3, sib, fbuf, pan, tabs, mown, mx, mfour, my,
     hsend, hrecv, fsend, frecv,
     child_sem, front_sem, out_sem, send_sem, recv_sem, sib_ssem, sib_rsem,
     m_ssem, m_rsem, h_ssem, h_rsem, f_ssem, f_rsem,
@@ -54,54 +54,73 @@
         )
 
     front_in = pltpu.make_async_copy(front, fbuf, front_sem)
-    for n, (_, _, r0, rows) in enumerate(CHUNKS):
-
-        def load(g, carry, n=n, r0=r0, rows=rows):
+
+    def load_group(g):
+        r0, rows = SPANS[g]
+
+        def load(i, carry):
             pltpu.make_async_copy(
-                child.at[g, pl.ds(r0, rows)],
-                buf.at[pl.ds(r0, rows), pl.ds(pl.multiple_of(g * 8, 8), 8), :],
-                child_sem.at[n],
+                child.at[i, pl.ds(r0, rows)],
+                buf.at[pl.ds(r0, rows), pl.ds(pl.multiple_of(i * 8, 8), 8), :],
+                child_sem.at[g],
             ).start()
             return carry
 
         lax.fori_loop(0, SLOTS // 8, load, 0)
-    front_in.start()
-
+
+    line_to = [
+        (i, (((x + i // 2) % 4) * 8 + z * 2 + (core + i) % 2, y)) for i in range(1, 8)
+    ]
+    plane_to = [
+        (i, (x * 8 + ((z + i // 4) % 4) * 2 + core, (y + i) % 4)) for i in range(1, 16)
+    ]
     barrier = pltpu.get_barrier_semaphore()
-    for axis in range(3):
-        for shift in (1, 2, 3):
-            pl.semaphore_signal(barrier, inc=1, device_id=peer(axis, shift), device_id_type=MESH)
-    pl.semaphore_signal(barrier, inc=1, device_id=sibling, device_id_type=MESH)
-    pl.semaphore_wait(barrier, 10)
-
+    for _, to in line_to + plane_to:
+        pl.semaphore_signal(barrier, inc=1, device_id=to, device_id_type=MESH)
+
+    sub16 = lax.broadcasted_iota(jnp.int32, (16, 128), 0)
+    lan16 = lax.broadcasted_iota(jnp.int32, (16, 128), 1)
+    line = jnp.zeros((8, 128), F32)
+    for a in range(6):
+        here_a = jnp.broadcast_to(mask[a].astype(F32), (8, 16)).astype(BF16)
+        spread = jnp.where(lan16 == sub16 + a * 16, 1.0, 0.0).astype(BF16)
+        line = line + jnp.dot(here_a, spread, preferred_element_type=F32)
     sub8 = lax.broadcasted_iota(jnp.int32, (8, 128), 0)
-    mown[...] = jnp.where(sub8 == x * 2 + core, jnp.broadcast_to(mask_row[0:1, :], (8, 128)), 0.0)
-    copy = remote(mown, mcore, m_ssem.at[0], m_rsem.at[0], sibling)
-    copy.start()
-    copy.wait()
-    mtwo[...] = mown[...] + mcore[...]
-    copies = [
-        remote(mtwo, mx.at[s - 1], m_ssem.at[s], m_rsem.at[s], peer(0, s)) for s in (1, 2, 3)
-    ]
+    mown[...] = jnp.where(sub8 == x * 2 + core, line, 0.0)
+    load_group(0)
+    pl.semaphore_wait(barrier, 22)
+    copies = [remote(mown, mx.at[i - 1], m_ssem.at[i], m_rsem.at[i], to) for i, to in line_to]
     for c in copies:
         c.start()
+    load_group(1)
     for c in copies:
         c.wait()
-    mfour[...] = mtwo[...] + mx[0] + mx[1] + mx[2]
-    mz[pl.ds(z, 1)] = mfour[...].reshape(1, 8, 128)
-    for s in (1, 2, 3):
-        remote(mfour, mz.at[z], m_ssem.at[3 + s], m_rsem.at[3 + s], peer(1, s)).start()
-    for s in (1, 2, 3):
-        remote(mfour, mz.at[(z + 4 - s) % 4], m_ssem.at[3 + s], m_rsem.at[3 + s], peer(1, s)).wait()
-    my[pl.ds(y, 1)] = mz[...].reshape(1, 4, 8, 128)
-    for s in (1, 2, 3):
-        remote(mz, my.at[y], m_ssem.at[6 + s], m_rsem.at[6 + s], peer(2, s)).start()
-    for s in (1, 2, 3):
-        remote(mz, my.at[(y + 4 - s) % 4], m_ssem.at[6 + s], m_rsem.at[6 + s], peer(2, s)).wait()
+    gathered = mown[...]
+    for i in range(7):
+        gathered = gathered + mx[i]
+    mfour[...] = gathered
+    my[pl.ds(y, 1), pl.ds(z, 1)] = gathered.reshape(1, 1, 8, 128)
+    for i, to in plane_to:
+        remote(mfour, my.at[y, z], m_ssem.at[7 + i], m_rsem.at[7 + i], to).start()
+    for g in range(2, N_GROUPS):
+        load_group(g)
+    front_in.start()
+    for i, to in plane_to:
+        at = my.at[(y + 16 - i) % 4, (z + 4 - i // 4) % 4]
+        remote(mfour, at, m_ssem.at[7 + i], m_rsem.at[7 + i], to).wait()
     masks = my[...].reshape(128, 128).astype(BF16)
 
-    own = owner[...]
-    at = slot[...]
+    sub = lax.broadcasted_iota(jnp.int32, (SLOTS, SLOTS), 0)
+    lan = lax.broadcasted_iota(jnp.int32, (SLOTS, SLOTS), 1)
+    eye = sub == lan
+    sub_f = sub.astype(F32)
+
+    def to_col(line):
+        values = jnp.where(eye, line.astype(F32), 0.0)
+        return jnp.sum(values, axis=1, keepdims=True).astype(jnp.int32)
+
+    own = to_col(owner[...])
+    at = to_col(slot[...])
     e = (own & 3) * 32 + ((own >> 3) & 3) * 8 + ((own >> 5) & 3) * 2 + ((own >> 2) & 1)
     lanes = lax.broadcasted_iota(jnp.int32, (SLOTS, 128), 1)
     by_owner = jnp.where(e == lanes, 1.0, 0.0).astype(BF16)
@@ -109,11 +128,6 @@
     keep = jnp.sum(jnp.where(at == lanes, keeps, 0.0), axis=1, keepdims=True)
     keep = jnp.where((at & 15) == 0, 1.0, keep)
     code = jnp.where(keep > 0.5, (e * 128 + at).astype(F32), -1.0)
-
-    sub = lax.broadcasted_iota(jnp.int32, (SLOTS, SLOTS), 0)
-    lan = lax.broadcasted_iota(jnp.int32, (SLOTS, SLOTS), 1)
-    eye = sub == lan
-    sub_f = sub.astype(F32)
 
     def to_row(col):
         return jnp.sum(jnp.where(eye, col, 0.0), axis=0, keepdims=True)
@@ -157,7 +171,8 @@
         return jnp.concatenate([hsend[phase, p, 0:CAP, 0:1], hrecv[phase, p, :, 0:1]], axis=0)
 
     overs = []
-    for p in range(3):
+
+    def first_table(p):
         table, passed, over = route(code, AXES[p][0])
         tabs[0, p] = table
         overs.append(over)
@@ -194,9 +209,10 @@
 
     def chunk_wait(phase, n, r0, rows):
         if phase == 0:
-            pltpu.make_async_copy(
-                buf.at[pl.ds(r0, rows)], buf.at[pl.ds(r0, rows)], child_sem.at[n]
-            ).wait()
+            g, p = CHUNKS[n][:2]
+            if p == 0:
+                ref = buf.at[pl.ds(SPANS[g][0], SPANS[g][1])]
+                pltpu.make_async_copy(ref, ref, child_sem.at[g]).wait()
         else:
             ref = recvs[phase].at[pl.ds(r0, rows)]
             remote(ref, ref, send_sem.at[phase - 1, n], recv_sem.at[phase - 1, n], sibling).wait_recv()
@@ -207,20 +223,19 @@
         table = tabs[phase, p]
 
         def body(it, carry):
-            for h in range(2):
-                i = r0 + it * 4 + h * 2
-                both = jnp.concatenate([rows_of(phase, i), rows_of(phase, i + 1)], axis=1)
-                got = split_dot(table, both)
-                for k in range(2):
-                    part = got[:, k * 128:(k + 1) * 128]
-                    if phase == 0:
-                        buf[i + k] = part
-                    else:
-                        buf[i + k, 0:CAP, :] = part[0:CAP]
-                        recvs[phase][i + k] = part[CAP:]
+            i = r0 + it * 2
+            both = jnp.concatenate([rows_of(phase, i), rows_of(phase, i + 1)], axis=1)
+            got = split_dot(table, both)
+            for k in range(2):
+                part = got[:, k * 128:(k + 1) * 128]
+                if phase == 0:
+                    buf[i + k] = part
+                else:
+                    buf[i + k, 0:CAP, :] = part[0:CAP]
+                    recvs[phase][i + k] = part[CAP:]
             return carry
 
-        lax.fori_loop(0, rows // 4, body, 0)
+        lax.fori_loop(0, rows // 2, body, 0)
         for s in (1, 2, 3):
             if phase == 0:
                 src = buf.at[pl.ds(r0, rows), pl.ds(s * CAP, CAP), :]
@@ -240,18 +255,17 @@
         table = tabs[3, p]
 
         def body(it, carry):
-            for h in range(2):
-                i = r0 + it * 4 + h * 2
-                both = jnp.concatenate([rows_of(3, i), rows_of(3, i + 1)], axis=1)
-                got = split_dot(table, both)
-                for k in range(2):
-                    part = got[:, k * 128:(k + 1) * 128]
-                    recv3[i + k, 0:96, :] = part[0:96]
-                    for a in range(6):
-                        fbuf[a, i + k] = fbuf[a, i + k] + part[96 + a * 16:112 + a * 16]
+            i = r0 + it * 2
+            both = jnp.concatenate([rows_of(3, i), rows_of(3, i + 1)], axis=1)
+            got = split_dot(table, both)
+            for k in range(2):
+                part = got[:, k * 128:(k + 1) * 128]
+                recv3[i + k, 0:96, :] = part[0:96]
+                for a in range(6):
+                    fbuf[a, i + k] = fbuf[a, i + k] + part[96 + a * 16:112 + a * 16]
             return carry
 
-        lax.fori_loop(0, rows // 4, body, 0)
+        lax.fori_loop(0, rows // 2, body, 0)
         remote(
             recv3.at[pl.ds(r0, rows), pl.ds(0, 96), :],
             sib.at[pl.ds(r0, rows)],
@@ -454,6 +468,8 @@
             if g == 0 and stage > 0:
                 later_tables(stage)
             for n in chunks:
+                if stage == 0 and g == 0:
+                    first_table(CHUNKS[n][1])
                 forward(stage, n)
         elif stage == 3:
             if g == 0:
@@ -479,7 +495,7 @@
             flag_step(flags_done)
             flags_done += 1
     flag_last.wait()
-    flag[...] = fsend[3] + frecv[3, 0]
+    flag[0, 0] = jnp.max(fsend[3] + frecv[3, 0]).astype(jnp.int32)
     for n, (_, _, r0, rows) in enumerate(CHUNKS):
         for phase in range(3):
             ref = recvs[phase + 1].at[pl.ds(r0, rows)]
@@ -493,7 +509,7 @@
         panel_end(g)
 
 
-def exchange(child, front, owner, slot, mask_row):
+def exchange(child, front, owner, slot, mask):
     dma = pltpu.SemaphoreType.DMA
     vmem = pl.BlockSpec(memory_space=pltpu.VMEM)
     hbm = pl.BlockSpec(memory_space=pl.ANY)
@@ -503,10 +519,10 @@
             jax.ShapeDtypeStruct((6, 128, 16, 128), F32),
             jax.ShapeDtypeStruct((4, 6, 128, 128), F32),
             jax.ShapeDtypeStruct((8, 4, 2, 128, 128), F32),
-            jax.ShapeDtypeStruct((8, 128), F32),
+            jax.ShapeDtypeStruct((1, 1), jnp.int32),
         ),
         in_specs=[hbm, hbm, vmem, vmem, vmem],
-        out_specs=(hbm, hbm, hbm, vmem),
+        out_specs=(hbm, hbm, hbm, pl.BlockSpec(memory_space=pltpu.SMEM)),
         scratch_shapes=[
             pltpu.VMEM((128, SLOTS, 128), F32),
             pltpu.VMEM((128, 3 * CAP, 128), F32),
@@ -517,25 +533,22 @@
             pltpu.VMEM((6, 128, 128), F32),
             pltpu.VMEM((4, 3, SLOTS, SLOTS), BF16),
             pltpu.VMEM((8, 128), F32),
+            pltpu.VMEM((7, 8, 128), F32),
             pltpu.VMEM((8, 128), F32),
-            pltpu.VMEM((8, 128), F32),
-            pltpu.VMEM((3, 8, 128), F32),
-            pltpu.VMEM((8, 128), F32),
-            pltpu.VMEM((4, 8, 128), F32),
             pltpu.VMEM((4, 4, 8, 128), F32),
             pltpu.VMEM((3, 3, SLOTS, 128), F32),
             pltpu.VMEM((3, 3, 3 * CAP, 128), F32),
             pltpu.VMEM((4, 8, 128), F32),
             pltpu.VMEM((4, 3, 8, 128), F32),
-            dma((N_CHUNKS,)),
+            dma((N_GROUPS,)),
             dma,
             dma((N_CHUNKS,)),
             dma((3, N_CHUNKS)),
             dma((3, N_CHUNKS)),
             dma((N_CHUNKS,)),
             dma((N_CHUNKS,)),
-            dma((10,)),
-            dma((10,)),
+            dma((23,)),
+            dma((23,)),
             dma((3, 3)),
             dma((3, 3)),
             dma((4, 3)),
@@ -554,7 +567,7 @@
             collective_id=0, has_side_effects=True, vmem_limit_bytes=62 * 2**20
         ),
         name="tile_exchange",
-    )(child, front, owner, slot, mask_row)
+    )(child, front, owner, slot, mask)
 
 
 def schur_kernel(
@@ -724,17 +737,16 @@
 def per_device(front, mask, child_tiles, owner_map, parent_slot, pivot_order, inv_pivot):
     child4 = child_tiles.reshape(24, 8, 128, 128).transpose(0, 2, 1, 3)
     mask_here = mask.reshape(6, 16)
-    mask_row = jnp.pad(mask.reshape(1, 96).astype(F32), ((0, 7), (0, 32)))
     assembled, panel, trail, flag = exchange(
         child4,
         front.reshape(6, 128, 16, 128),
-        owner_map.reshape(192, 1),
-        parent_slot.reshape(192, 1),
-        mask_row,
+        owner_map.reshape(1, 192),
+        parent_slot.reshape(1, 192),
+        mask.reshape(6, 1, 16),
     )
     col_at = lax.axis_index("col").astype(jnp.int32).reshape(1)
     return lax.cond(
-        flag[0, 0] > 0.5,
+        flag[0, 0] > 0,
         lambda: any_front(
             front, mask, child_tiles, owner_map, parent_slot, pivot_order, inv_pivot
         ),

time: 248 us -> 232 us (0.935)
  Pallas kernels: 228 us -> 218 us
  local copies, waits for them, and re-layouts: 4.76 us -> 0.02 us
    pallas_call x1, Pallas kernels: 212 us -> 202 us  [exchange(): pl.pallas_call(exchange_kernel, out_shape=(jax.ShapeDtypeStruct((6, 128,...]
where the time goes in v1:
time: 232 us
  Pallas kernels  218 us (94%)
  between operations  14 us (6%)
    pallas_call x1, Pallas kernels, exchange(): pl.pallas_call(exchange_kernel, out_shape=(jax.ShapeDtypeStruct((6, 128,...  202 us
    pallas_call x1, Pallas kernels, finish_front(): pl.pallas_call(schur_kernel, grid=(3,), out_shape=jax.ShapeDtypeStruct((1...  16.3 us

profile of v1, /device:TPU:1, one launch (start us, length us, event | category | flops | bytes accessed | tf_op | source)
XLA Modules:
  0.0 232.0 jit_solution(13452273035416793050)
XLA Ops:
  6.5 0.0 copy-start.2
  6.5 0.0 copy-start.4
  6.5 0.0 copy-start.5
  6.5 0.0 copy-start.6
  6.5 201.6 %tile_exchange.1 = (f32[6,128,16,128]{3,2,1,0:T(8,128)}, f32[4,6,128,128]{3,2,1,0:T(8,128)}, f32[8,4,2,128,128]{4,3,2,1,0:T(8,128)}, s32[1,1]{1,0:T(1,128)}) custom-call(f32[24,128,8,128]{3,2,1,0:T(8,128)} %bitcast.82, f32[6,128,16,128]{3,2,1,0:T(8,128)} %bitcast.75, s32[1,192]{1,0:T(1,128)} %bitcast.95, s32[1,192]{1,0:T(1,128)} %bitcast.102, ...), custom_call_target="tpu_custom_call" | custom-call | tf_op jit(solution)/shard_map/tile_exchange/pallas_call | solution.py:516
  208.8 0.0 copy-done.2
  208.8 0.0 copy-done.4
  208.8 0.0 copy-done.5
  208.8 0.0 copy-done.6
  208.8 16.3 %conditional.1 = (f32[6,1,128,16,1,128]{5,3,2,0,4,1:T(8,128)}) conditional(s32[]{:T(128)} %bitcast.29, (s32[512]{0:T(512)S(1)}, f32[6,128,16,128]{3,2,1,0:T(8,128)}, s32[]{:T(128)}, s32[6,1,16,1]{2,3,1,0:T(1,128)S(1)}, f32[512,512]{1,0:T(8,128)S(1)}, /*index=5*/f32[4,6,128,128]{3,2,1,0:T(8,128)}, f32[8,4,2,128,128]{4,3,2,1,0:T(8,128)}) %tuple.33, ...), branch_computations={%region_0.0_spmd, %region_1.8_spmd} | conditional | flops 11491074048 | bytes 445776736 | solution.py:748
  208.9 16.3 %schur.1 = f32[12288,128]{1,0:T(8,128)} custom-call(s32[1]{0:T(128)} %bitcast.col_at, s32[6,16]{1,0:T(8,128)S(1)} %bitcast.70, s32[1,512]{1,0:T(1,128)S(1)} %bitcast.92, f32[512,512]{1,0:T(8,128)S(1)} %get-tuple-element.39.inverse, f32[4,6,128,128]{3,2,1,0:T(8,128)} %get-tuple-element.40.panel, f32[8,4,2,128,128]{4,3,2,1,0:T(8,128)} %get-tuple-element.41.trail, ...), custom_call_target="tpu_custom_call" | custom-call | tf_op jit(solution)/shard_map/cond/branch_0_fun/schur/pallas_call | solution.py:633
  (1 shorter events, 0.0 us)
Async XLA Ops:
  6.5 202.3 %copy-start.2 = (f32[512,512]{1,0:T(8,128)S(1)}, f32[512,512]{1,0:T(8,128)}, u32[]{:S(2)}) copy-start(f32[512,512]{1,0:T(8,128)} %param.15) | copy-start | bytes 3145732
  6.5 202.3 %copy-start.4 = (s32[6,1,16,1]{2,3,1,0:T(1,128)S(1)}, s32[6,1,16,1]{2,3,1,0:T(1,128)}, u32[]{:S(2)}) copy-start(s32[6,1,16,1]{2,3,1,0:T(1,128)} %param.10) | copy-start | bytes 1156
  6.5 202.3 %copy-start.5 = (s32[512]{0:T(512)S(1)}, s32[512]{0:T(512)}, u32[]{:S(2)}) copy-start(s32[512]{0:T(512)} %param.14) | copy-start | bytes 6148
  6.5 202.3 %copy-start.6 = (s32[192,1]{0,1:T(1,128)S(1)}, s32[192,1]{0,1:T(1,128)}, u32[]{:S(2)}) copy-start(s32[192,1]{0,1:T(1,128)} %param.12) | copy-start | bytes 2308

commit v2 on v1

--- a/solution.py
+++ b/solution.py
@@ -370,6 +370,14 @@
         ref = trail_at(g, 2 * at + zz, 1)
         return remote(ref, ref, b_ssem.at[g, 1 + zz, s - 1], b_rsem.at[g, 1 + zz, s - 1], peer(0, s))
 
+    def relayed(g):
+        return g < N_GROUPS - 2
+
+    def relay(g, i, base):
+        place = 2 * i + base // 2
+        ref = trail_at(g, place, 0)
+        return remote(ref, ref, a_ssem.at[g, 1 + i, 1], a_rsem.at[g, 1 + i, 1], peer(1, 1 if i < 2 else 3))
+
     def panel_lines(g):
         @pl.when(source)
         def _():
@@ -378,7 +386,7 @@
             for s in (1, 2, 3):
                 source_copy(g, 0, a_sems, s, from_x(s) + z // 2).wait_recv()
             for i in range(4):
-                for s in (1, 3, 2):
+                for s in (1, 3) if relayed(g) else (1, 3, 2):
                     a_line(g, s, i, z).start()
             source_copy(g, 1, b_sems, 2, other).wait_recv()
 
@@ -399,22 +407,29 @@
         return remote(ref, ref, c_ssem.at[g], c_rsem.at[g], sibling)
 
     def panel_cores(g):
-        @pl.when(source)
-        def _():
-            for i in range(4):
-                a_line(g, 2, i, (z + 2) % 4).wait_recv()
-
         @pl.when(off_line)
         def _():
             for i in range(4):
                 for s in (1, 3):
                     a_line(g, s, i, (z + 4 - s) % 4).wait_recv()
+            if relayed(g):
+                for i in range(4):
+                    relay(g, i, (z + 3) % 4 if i < 2 else (z + 1) % 4).start()
 
         @pl.when(holds)
         def _():
             for zz in (0, 1):
                 for s in (1, 2, 3):
                     b_line(g, s, zz, (x + 4 - s) % 4).wait_recv()
+
+    def panel_ends(g):
+        @pl.when(source)
+        def _():
+            for i in range(4):
+                a_line(g, 2, i, (z + 2) % 4).wait_recv()
+
+        @pl.when(holds)
+        def _():
             to_sibling(g).start()
 
     def panel_end(g):
@@ -427,8 +442,15 @@
                 for s in (1, 2, 3):
                     source_copy(g, half, (a_sems, b_sems)[half], s, mine).wait_send()
             for i in range(4):
-                for s in (1, 2, 3):
+                for s in (1, 3) if relayed(g) else (1, 2, 3):
                     a_line(g, s, i, z).wait_send()
+
+        if relayed(g):
+
+            @pl.when(off_line)
+            def _():
+                for i in range(4):
+                    relay(g, i, (z + 3) % 4 if i < 2 else (z + 1) % 4).wait_send()
 
         @pl.when(holds)
         def _():
@@ -461,7 +483,7 @@
             c.start()
 
     flags_done = 0
-    steps = sorted((stage + g, stage, g) for stage in range(8) for g in range(N_GROUPS))
+    steps = sorted((stage + g, stage, g) for stage in range(9) for g in range(N_GROUPS))
     for _, stage, g in steps:
         chunks = [n for n in range(N_CHUNKS) if CHUNKS[n][0] == g]
         if stage < 3:
@@ -489,8 +511,10 @@
             panel_rows(g)
         elif stage == 6:
             panel_lines(g)
+        elif stage == 7:
+            panel_cores(g)
         else:
-            panel_cores(g)
+            panel_ends(g)
         if stage >= 3 and flags_done < 4:
             flag_step(flags_done)
             flags_done += 1

time: 232 us -> 231 us (level)
  no operation moved by 1% of the time
where the time goes in v2:
time: 231 us
  Pallas kernels  217 us (94%)
  between operations  14 us (6%)
    pallas_call x1, Pallas kernels, exchange(): pl.pallas_call(exchange_kernel, out_shape=(jax.ShapeDtypeStruct((6, 128,...  201 us
    pallas_call x1, Pallas kernels, finish_front(): pl.pallas_call(schur_kernel, grid=(3,), out_shape=jax.ShapeDtypeStruct((1...  16.3 us

profile of v2, /device:TPU:1, one launch (start us, length us, event | category | flops | bytes accessed | tf_op | source)
XLA Modules:
  0.0 231.0 jit_solution(8242520395143748250)
XLA Ops:
  6.5 0.0 copy-start.2
  6.5 0.0 copy-start.4
  6.5 0.0 copy-start.5
  6.5 0.0 copy-start.6
  6.5 200.7 %tile_exchange.1 = (f32[6,128,16,128]{3,2,1,0:T(8,128)}, f32[4,6,128,128]{3,2,1,0:T(8,128)}, f32[8,4,2,128,128]{4,3,2,1,0:T(8,128)}, s32[1,1]{1,0:T(1,128)}) custom-call(f32[24,128,8,128]{3,2,1,0:T(8,128)} %bitcast.82, f32[6,128,16,128]{3,2,1,0:T(8,128)} %bitcast.75, s32[1,192]{1,0:T(1,128)} %bitcast.95, s32[1,192]{1,0:T(1,128)} %bitcast.102, ...), custom_call_target="tpu_custom_call" | custom-call | tf_op jit(solution)/shard_map/tile_exchange/pallas_call | solution.py:540
  207.8 0.0 copy-done.2
  207.8 0.0 copy-done.4
  207.8 0.0 copy-done.5
  207.9 0.0 copy-done.6
  207.9 16.3 %conditional.1 = (f32[6,1,128,16,1,128]{5,3,2,0,4,1:T(8,128)}) conditional(s32[]{:T(128)} %bitcast.29, (s32[512]{0:T(512)S(1)}, f32[6,128,16,128]{3,2,1,0:T(8,128)}, s32[]{:T(128)}, s32[6,1,16,1]{2,3,1,0:T(1,128)S(1)}, f32[512,512]{1,0:T(8,128)S(1)}, /*index=5*/f32[4,6,128,128]{3,2,1,0:T(8,128)}, f32[8,4,2,128,128]{4,3,2,1,0:T(8,128)}) %tuple.33, ...), branch_computations={%region_0.0_spmd, %region_1.8_spmd} | conditional | flops 11491074048 | bytes 445776736 | solution.py:772
  207.9 16.3 %schur.1 = f32[12288,128]{1,0:T(8,128)} custom-call(s32[1]{0:T(128)} %bitcast.col_at, s32[6,16]{1,0:T(8,128)S(1)} %bitcast.70, s32[1,512]{1,0:T(1,128)S(1)} %bitcast.92, f32[512,512]{1,0:T(8,128)S(1)} %get-tuple-element.39.inverse, f32[4,6,128,128]{3,2,1,0:T(8,128)} %get-tuple-element.40.panel, f32[8,4,2,128,128]{4,3,2,1,0:T(8,128)} %get-tuple-element.41.trail, ...), custom_call_target="tpu_custom_call" | custom-call | tf_op jit(solution)/shard_map/cond/branch_0_fun/schur/pallas_call | solution.py:657
  (1 shorter events, 0.0 us)
Async XLA Ops:
  6.5 201.3 %copy-start.2 = (f32[512,512]{1,0:T(8,128)S(1)}, f32[512,512]{1,0:T(8,128)}, u32[]{:S(2)}) copy-start(f32[512,512]{1,0:T(8,128)} %param.15) | copy-start | bytes 3145732
  6.5 201.3 %copy-start.4 = (s32[6,1,16,1]{2,3,1,0:T(1,128)S(1)}, s32[6,1,16,1]{2,3,1,0:T(1,128)}, u32[]{:S(2)}) copy-start(s32[6,1,16,1]{2,3,1,0:T(1,128)} %param.10) | copy-start | bytes 1156
  6.5 201.3 %copy-start.5 = (s32[512]{0:T(512)S(1)}, s32[512]{0:T(512)}, u32[]{:S(2)}) copy-start(s32[512]{0:T(512)} %param.14) | copy-start | bytes 6148
  6.5 201.3 %copy-start.6 = (s32[192,1]{0,1:T(1,128)S(1)}, s32[192,1]{0,1:T(1,128)}, u32[]{:S(2)}) copy-start(s32[192,1]{0,1:T(1,128)} %param.12) | copy-start | bytes 2308
